TPU v7x, 256 devices: a whole 4x4x8 slice. The times are simulated.
256 devices in a mesh: section: 2 (over core), row: 8 (over z), col: 16 (over y, x).
Axes of the slice: x: 4, y: 4, z: 8, core: 2. Of those that a mesh axis runs over, the one named last changes fastest.
Arguments:
- hidden_in: bfloat16 [2, 1024, 8192], P('section', 'col', 'row'), may hold values from -80 to 80
- norm_gain: float32 [2, 8192], P('section', 'row'), may hold values from 0.1 to 1.9
- gate_saved: bfloat16 [2, 1024, 14336], P('section', 'row', 'col'), may hold values from -6 to 6
- up_saved: bfloat16 [2, 1024, 14336], P('section', 'row', 'col'), may hold values from -6 to 6
- w_gate: bfloat16 [2, 8192, 14336], P('section', 'row', 'col'), may hold values from -0.0625 to 0.0625
- w_up: bfloat16 [2, 8192, 14336], P('section', 'row', 'col'), may hold values from -0.0625 to 0.0625
- w_down: bfloat16 [2, 14336, 8192], P('section', 'col', 'row'), may hold values from -0.046875 to 0.046875
- out_grad: bfloat16 [1024, 8192], P('col', 'row'), may hold values from -6 to 6
Outputs:
- in_grad: bfloat16 [2, 1024, 8192], P('section', 'col', 'row')
- gain_grad: float32 [2, 8192], P('section', 'row')
- grad_gate: bfloat16 [2, 8192, 14336], P('section', 'row', 'col')
- grad_up: bfloat16 [2, 8192, 14336], P('section', 'row', 'col')
- grad_down: bfloat16 [2, 14336, 8192], P('section', 'col', 'row')
All inputs are finite; a program needn't handle non-finite values.
Results may differ from a plain program's by a relative error of at most 0.03.
Values may be sent and summed in bfloat16 or wider, within the bound.
No kernel may reach another device: no remote copies, remote signals or barrier semaphores. Data moves between devices by JAX's collectives and lax.ppermute only.
A program may use at most 128 MiB of HBM per device.

v0:
```python
import jax
import jax.numpy as jnp
from jax import lax
from jax.sharding import PartitionSpec as P

D = 8192


epsilon = 1e-05


def passed_along(block, axis, distance):
    devices = range(lax.axis_size(axis))
    route = [(i - distance, i) for i in devices if i - distance in devices]
    return lax.ppermute(block, axis, route)


def contract_cols(left, right):
    return lax.dot_general(
        left, right, (((1,), (1,)), ((), ())), preferred_element_type=jnp.float32
    )


def contract_rows(left, right):
    return lax.dot_general(
        left, right, (((0,), (0,)), ((), ())), preferred_element_type=jnp.float32
    )


def silu_grads(hidden_grad, gate_pre, up_vals):
    gate_f = gate_pre.astype(jnp.float32)
    up_f = up_vals.astype(jnp.float32)
    sig = jax.nn.sigmoid(gate_f)
    gate_grad = (hidden_grad * up_f * sig * (1.0 + gate_f * (1.0 - sig))).astype(jnp.bfloat16)
    up_grad = (hidden_grad * gate_f * sig).astype(jnp.bfloat16)
    return (gate_grad, up_grad)


def activation(gate_pre, up_vals):
    gate_f = gate_pre.astype(jnp.float32)
    return (gate_f * jax.nn.sigmoid(gate_f) * up_vals.astype(jnp.float32)).astype(jnp.bfloat16)


def body(hidden_in, norm_gain, gate_saved, up_saved, w_gate, w_up, w_down, out_grad):
    hidden = hidden_in[0]
    hidden_f = hidden.astype(jnp.float32)
    gain = norm_gain[0]
    gate_pre = gate_saved[0]
    up_local = up_saved[0]
    gate_w = w_gate[0]
    up_w = w_up[0]
    down_w = w_down[0]
    section_index = lax.axis_index("section")
    squares = jnp.sum(hidden_f * hidden_f, axis=1)
    square_total = lax.psum(squares, "row")

    def backward_data(cotangent):
        cot_full = lax.all_gather(cotangent, "col", axis=0, tiled=True)
        hidden_grad = lax.psum_scatter(
            contract_cols(cot_full, down_w).astype(jnp.bfloat16),
            "row",
            scatter_dimension=0,
            tiled=True,
        ).astype(jnp.float32)
        gate_grad, up_grad = silu_grads(hidden_grad, gate_pre, up_local)
        gate_grads, up_grads = (
            lax.all_gather(gate_grad, "row", axis=0, tiled=True),
            lax.all_gather(up_grad, "row", axis=0, tiled=True),
        )
        normed_grad = lax.psum_scatter(
            (contract_cols(gate_grads, gate_w) + contract_cols(up_grads, up_w)).astype(
                jnp.bfloat16
            ),
            "col",
            scatter_dimension=0,
            tiled=True,
        ).astype(jnp.float32)
        cross = jnp.sum(gain * normed_grad * hidden_f, axis=1)
        cross = lax.psum(cross, "row")
        inv_rms = lax.rsqrt(square_total / D + epsilon)
        result = (
            cotangent.astype(jnp.float32)
            + inv_rms[:, None] * gain * normed_grad
            - hidden_f * (inv_rms**3 * cross / D)[:, None]
        ).astype(jnp.bfloat16)
        return (result, normed_grad, inv_rms, cot_full, gate_grads, up_grads)

    first_pass = backward_data(out_grad)[0]
    received = passed_along(first_pass, "section", -1)
    cotangent = jnp.where(section_index == 0, received, out_grad)
    result, normed_grad, inv_rms, cot_full, gate_grads, up_grads = backward_data(cotangent)
    down_total = contract_rows(
        lax.all_gather(activation(gate_pre, up_local), "row", axis=0, tiled=True), cot_full
    )
    normed_local = (hidden_f * inv_rms[:, None] * gain).astype(jnp.bfloat16)
    piece = lax.all_gather(normed_local, "col", axis=0, tiled=True)
    gate_total = contract_rows(piece, gate_grads)
    up_total = contract_rows(piece, up_grads)
    gain_total = lax.psum(jnp.sum(normed_grad * hidden_f * inv_rms[:, None], axis=0), "col")
    return (
        result[None],
        gain_total[None],
        gate_total.astype(jnp.bfloat16)[None],
        up_total.astype(jnp.bfloat16)[None],
        down_total.astype(jnp.bfloat16)[None],
    )


def solution(mesh):
    placed = (
        P("section", "col", "row"),
        P("section", "row"),
        P("section", "row", "col"),
        P("section", "row", "col"),
        P("section", "row", "col"),
        P("section", "row", "col"),
        P("section", "col", "row"),
        P("col", "row"),
    )
    return jax.shard_map(
        body,
        mesh=mesh,
        in_specs=placed,
        out_specs=(
            P("section", "col", "row"),
            P("section", "row"),
            P("section", "row", "col"),
            P("section", "row", "col"),
            P("section", "col", "row"),
        ),
        check_vma=False,
    )
```

profile of v0, /device:TPU:1, one launch (start us, length us, event | category | flops | bytes accessed | tf_op | source)
XLA Modules:
  0.0 674.0 jit_solution(10657821731467751767)
XLA Ops:
  7.2 0.0 copy-start
  7.2 0.0 all-gather.9.cloned.1.call-start
  7.2 0.7 all-gather.9.cloned.1.call-update
  7.9 0.0 reduce-scatter.5.cloned.1.call-start
  8.0 55.4 %all-gather.9.cloned.1.call-done = bf16[1024,1024]{1,0:T(8,128)(2,1)} async-done(((bf16[64,1024]{1,0:T(8,128)(2,1)}), bf16[1024,1024]{1,0:T(8,128)(2,1)}) %all-gather.9.cloned.1.call-update) | async-done | bytes 2097168 | tf_op jit(solution)/shard_map/all_gather | solution.py:58
  63.4 5.7 fusion.10
  69.1 0.0 reduce-scatter.5.cloned.1.call-update
  69.1 0.0 all-gather.11.cloned.1.call-start
  69.2 37.7 %reduce-scatter.5.cloned.1.call-done = bf16[128,896]{1,0:T(8,128)(2,1)} async-done(((bf16[1024,896]{1,0:T(8,128)(2,1)}), bf16[128,896]{1,0:T(8,128)(2,1)}) %reduce-scatter.5.cloned.1.call-update) | async-done | bytes 229392 | tf_op jit(solution)/shard_map/reduce_scatter | solution.py:59
  106.9 0.0 copy-done.4
  106.9 0.0 copy-done.5
  106.9 1.9 fusion.28
  108.8 0.0 all-gather.11.cloned.1.call-update
  108.8 0.0 all-gather.13.cloned.1.call-start
  108.9 0.5 all-gather.13.cloned.1.call-update
  109.4 0.0 reduce-scatter.7.cloned.1.call-start
  109.5 39.3 %all-gather.11.cloned.1.call-done = bf16[1024,896]{1,0:T(8,128)(2,1)} async-done(((bf16[128,896]{1,0:T(8,128)(2,1)}), bf16[1024,896]{1,0:T(8,128)(2,1)}) %all-gather.11.cloned.1.call-update) | async-done | bytes 1835024 | tf_op jit(solution)/shard_map/all_gather | solution.py:67
  148.8 0.0 copy-done
  148.8 5.8 fusion.4
  154.6 35.6 %all-gather.13.cloned.1.call-done = bf16[1024,896]{1,0:T(8,128)(2,1)} async-done(((bf16[128,896]{1,0:T(8,128)(2,1)}), bf16[1024,896]{1,0:T(8,128)(2,1)}) %all-gather.13.cloned.1.call-update) | async-done | bytes 1835024 | tf_op jit(solution)/shard_map/all_gather | solution.py:68
  190.2 7.0 %add_convert_fusion.1 = bf16[1024,1024]{1,0:T(8,128)(2,1)} fusion(f32[1024,1024]{1,0:T(8,128)} %fusion.4, bf16[1024,896]{1,0:T(8,128)(2,1)} %all-gather.13.cloned.1.call-done, bf16[1,1024,896]{2,1,0:T(8,128)(2,1)} %param.13), kind=kOutput, calls=%fused_computation.1 | convolution fusion | flops 1881145344 | bytes 9961472 | tf_op jit(solution)/shard_map/dot_general | solution.py:19
  197.2 0.0 reduce-scatter.7.cloned.1.call-update
  197.2 0.0 all-gather.15.cloned.1.call-start
  197.3 80.2 %reduce-scatter.7.cloned.1.call-done = bf16[64,1024]{1,0:T(8,128)(2,1)} async-done(((bf16[1024,1024]{1,0:T(8,128)(2,1)}), bf16[64,1024]{1,0:T(8,128)(2,1)}) %reduce-scatter.7.cloned.1.call-update) | async-done | bytes 131088 | tf_op jit(solution)/shard_map/reduce_scatter | solution.py:70
  277.4 0.0 copy-done.1
  277.4 0.0 copy-done.6
  277.4 1.1 fusion.37
  278.5 13.7 %all-reduce = (f32[64]{0:T(128)S(1)}, f32[64]{0:T(128)S(1)}) all-reduce(f32[64]{0:T(128)S(1)} %get-tuple-element.8, f32[64]{0:T(128)S(1)} %get-tuple-element.7), channel_id=1, replica_groups=mesh['section'=2,'row'=8,'col'=16] {'row'}, use_global_device_ids=true, to_apply=%region_5.0 | all-reduce | flops 128 | bytes 1024 | tf_op jit(solution)/shard_map/psum | solution.py:79
  292.3 1.1 fusion.33
  293.3 8.0 %collective-permute-start = (bf16[64,1024]{1,0:T(8,128)(2,1)S(1)}, bf16[64,1024]{1,0:T(8,128)(2,1)S(1)}, u32[]{:S(2)}, u32[]{:S(2)}) collective-permute-start(bf16[64,1024]{1,0:T(8,128)(2,1)S(1)} %fusion.33), channel_id=1, source_target_pairs={{128,0},{129,1},{130,2},{131,3},{132,4},{133,5},{134,6},{135,7},{1... | collective-permute-start | bytes 393224 | tf_op jit(solution)/shard_map/ppermute | solution.py:15
  301.3 1.0 collective-permute-done
  302.3 0.7 broadcast_select_fusion
  303.0 0.0 all-gather.15.cloned.1.call-update
  303.0 0.0 reduce-scatter.9.cloned.1.call-start
  303.0 45.6 %all-gather.15.cloned.1.call-done = bf16[1024,1024]{1,0:T(8,128)(2,1)} async-done(((bf16[64,1024]{1,0:T(8,128)(2,1)}), bf16[1024,1024]{1,0:T(8,128)(2,1)}) %all-gather.15.cloned.1.call-update) | async-done | bytes 2097168 | tf_op jit(solution)/shard_map/all_gather | solution.py:58
  348.6 5.7 fusion.13
  354.3 0.0 reduce-scatter.9.cloned.1.call-update
  354.3 0.0 all-gather.17.cloned.1.call-start
  354.4 37.6 %reduce-scatter.9.cloned.1.call-done = bf16[128,896]{1,0:T(8,128)(2,1)} async-done(((bf16[1024,896]{1,0:T(8,128)(2,1)}), bf16[128,896]{1,0:T(8,128)(2,1)}) %reduce-scatter.9.cloned.1.call-update) | async-done | bytes 229392 | tf_op jit(solution)/shard_map/reduce_scatter | solution.py:59
  392.0 2.0 fusion.22
  394.1 0.0 all-gather.17.cloned.1.call-update
  394.1 0.0 all-gather.19.cloned.1.call-start
  394.1 0.7 all-gather.19.cloned.1.call-update
  394.8 0.0 reduce-scatter.11.cloned.1.call-start
  394.9 39.3 %all-gather.17.cloned.1.call-done = bf16[1024,896]{1,0:T(8,128)(2,1)} async-done(((bf16[128,896]{1,0:T(8,128)(2,1)}), bf16[1024,896]{1,0:T(8,128)(2,1)}) %all-gather.17.cloned.1.call-update) | async-done | bytes 1835024 | tf_op jit(solution)/shard_map/all_gather | solution.py:67
  434.1 5.8 fusion.2
  440.0 35.9 %all-gather.19.cloned.1.call-done = bf16[1024,896]{1,0:T(8,128)(2,1)} async-done(((bf16[128,896]{1,0:T(8,128)(2,1)}), bf16[1024,896]{1,0:T(8,128)(2,1)}) %all-gather.19.cloned.1.call-update) | async-done | bytes 1835024 | tf_op jit(solution)/shard_map/all_gather | solution.py:68
  475.9 7.0 %add_convert_fusion = bf16[1024,1024]{1,0:T(8,128)(2,1)} fusion(f32[1024,1024]{1,0:T(8,128)} %fusion.2, bf16[1024,896]{1,0:T(8,128)(2,1)} %all-gather.19.cloned.1.call-done, bf16[1,1024,896]{2,1,0:T(8,128)(2,1)} %param.13), kind=kOutput, calls=%fused_computation | convolution fusion | flops 1881145344 | bytes 9961472 | tf_op jit(solution)/shard_map/dot_general | solution.py:19
  482.9 0.0 reduce-scatter.11.cloned.1.call-update
  482.9 0.0 all-gather.23.cloned.1.call-start
  482.9 0.7 all-gather.23.cloned.1.call-update
  483.6 0.0 all-gather.21.cloned.1.call-start
  483.7 79.4 %reduce-scatter.11.cloned.1.call-done = bf16[64,1024]{1,0:T(8,128)(2,1)} async-done(((bf16[1024,1024]{1,0:T(8,128)(2,1)}), bf16[64,1024]{1,0:T(8,128)(2,1)}) %reduce-scatter.11.cloned.1.call-update) | async-done | bytes 131088 | tf_op jit(solution)/shard_map/reduce_scatter | solution.py:70
  563.0 1.1 fusion.41
  564.2 13.9 %psum.30 = f32[64]{0:T(128)S(1)} all-reduce(f32[64]{0:T(128)S(1)} %get-tuple-element.6), channel_id=1, replica_groups=mesh['section'=2,'row'=8,'col'=16] {'row'}, use_global_device_ids=true, to_apply=%region_9.10 | all-reduce | flops 64 | bytes 512 | tf_op jit(solution)/shard_map/psum | solution.py:79
  578.1 1.8 fusion.43
  579.9 0.0 all-gather.21.cloned.1.call-update
  579.9 23.5 %all-gather.23.cloned.1.call-done = bf16[1024,896]{1,0:T(8,128)(2,1)} async-done(((bf16[128,896]{1,0:T(8,128)(2,1)}), bf16[1024,896]{1,0:T(8,128)(2,1)}) %all-gather.23.cloned.1.call-update) | async-done | bytes 1835024 | tf_op jit(solution)/shard_map/all_gather | solution.py:93
  603.4 5.5 convert_bitcast_fusion
  608.9 33.7 %psum.31 = f32[1,1024]{1,0:T(1,128)} all-reduce(f32[1,1024]{1,0:T(1,128)S(1)} %bitcast.77), channel_id=1, replica_groups=mesh['section'=2,'row'=8,'col'=16] {'col'}, use_global_device_ids=true, to_apply=%region_11.12 | all-reduce | flops 1024 | bytes 8192 | tf_op jit(solution)/shard_map/psum | solution.py:99
  642.6 15.0 %all-gather.21.cloned.1.call-done = bf16[1024,1024]{1,0:T(8,128)(2,1)} async-done(((bf16[64,1024]{1,0:T(8,128)(2,1)}), bf16[1024,1024]{1,0:T(8,128)(2,1)}) %all-gather.21.cloned.1.call-update) | async-done | bytes 2097168 | tf_op jit(solution)/shard_map/all_gather | solution.py:96
  657.6 5.9 convert_bitcast_fusion.1
  663.5 0.0 copy-done.7
  663.5 3.6 convert_bitcast_fusion.2
  (13 shorter events, 0.0 us)
Async XLA Ops:
  7.2 141.6 %copy-start = (bf16[1,1024,896]{2,1,0:T(8,128)(2,1)S(1)}, bf16[1,1024,896]{2,1,0:T(8,128)(2,1)}, u32[]{:S(2)}) copy-start(bf16[1,1024,896]{2,1,0:T(8,128)(2,1)} %param.12) | copy-start | bytes 5505028
  7.2 56.2 %all-gather.9.cloned.1.call-start = ((), (), s32[]{:S(2)}) async-start(), calls=%async_computation.4 | async-start | bytes 2228224 | tf_op jit(solution)/shard_map/all_gather | solution.py:58
  7.9 99.0 %reduce-scatter.5.cloned.1.call-start = ((), (), s32[]{:S(2)}) async-start(), calls=%async_computation.5 | async-start | bytes 2064384 | tf_op jit(solution)/shard_map/reduce_scatter | solution.py:59
  69.1 37.8 %copy-start.4 = (bf16[1,128,896]{2,1,0:T(8,128)(2,1)S(1)}, bf16[1,128,896]{2,1,0:T(8,128)(2,1)}, u32[]{:S(2)}) copy-start(bf16[1,128,896]{2,1,0:T(8,128)(2,1)} %param.10) | copy-start | bytes 688132
  69.1 37.8 %copy-start.5 = (bf16[1,128,896]{2,1,0:T(8,128)(2,1)S(1)}, bf16[1,128,896]{2,1,0:T(8,128)(2,1)}, u32[]{:S(2)}) copy-start(bf16[1,128,896]{2,1,0:T(8,128)(2,1)} %param.11) | copy-start | bytes 688132
  69.1 79.6 %all-gather.11.cloned.1.call-start = ((), (), s32[]{:S(2)}) async-start(), calls=%async_computation.6 | async-start | bytes 2064384 | tf_op jit(solution)/shard_map/all_gather | solution.py:67
  108.8 81.3 %all-gather.13.cloned.1.call-start = ((), (), s32[]{:S(2)}) async-start(), calls=%async_computation.7 | async-start | bytes 2064384 | tf_op jit(solution)/shard_map/all_gather | solution.py:68
  109.4 168.0 %reduce-scatter.7.cloned.1.call-start = ((), (), s32[]{:S(2)}) async-start(), calls=%async_computation.8 | async-start | bytes 2228224 | tf_op jit(solution)/shard_map/reduce_scatter | solution.py:70
  197.2 80.2 %copy-start.1 = (bf16[1,64,1024]{2,1,0:T(8,128)(2,1)S(1)}, bf16[1,64,1024]{2,1,0:T(8,128)(2,1)}, u32[]{:S(2)}) copy-start(bf16[1,64,1024]{2,1,0:T(8,128)(2,1)} %param.8) | copy-start | bytes 393220
  197.2 80.2 %copy-start.6 = (f32[1,1024]{1,0:T(1,128)S(1)}, f32[1,1024]{1,0:T(1,128)}, u32[]{:S(2)}) copy-start(f32[1,1024]{1,0:T(1,128)} %param.9) | copy-start | bytes 12292
  197.2 95.0 %copy-start.3 = (bf16[64,1024]{1,0:T(8,128)(2,1)S(1)}, bf16[64,1024]{1,0:T(8,128)(2,1)}, u32[]{:S(2)}) copy-start(bf16[64,1024]{1,0:T(8,128)(2,1)} %param.15) | copy-start | bytes 393220
  197.2 151.4 %all-gather.15.cloned.1.call-start = ((), (), s32[]{:S(2)}) async-start(), calls=%async_computation.9 | async-start | bytes 2228224 | tf_op jit(solution)/shard_map/all_gather | solution.py:58
  293.3 9.0 %collective-permute-start = (bf16[64,1024]{1,0:T(8,128)(2,1)S(1)}, bf16[64,1024]{1,0:T(8,128)(2,1)S(1)}, u32[]{:S(2)}, u32[]{:S(2)}) collective-permute-start(bf16[64,1024]{1,0:T(8,128)(2,1)S(1)} %fusion.33), channel_id=1, source_target_pairs={{128,0},{129,1},{130,2},{131,3},{132,4},{133,5},{134,6},{135,7},{1... | collective-permute-start | bytes 393224 | tf_op jit(solution)/shard_map/ppermute | solution.py:15
  303.0 89.0 %reduce-scatter.9.cloned.1.call-start = ((), (), s32[]{:S(2)}) async-start(), calls=%async_computation.10 | async-start | bytes 2064384 | tf_op jit(solution)/shard_map/reduce_scatter | solution.py:59
  354.3 79.8 %all-gather.17.cloned.1.call-start = ((), (), s32[]{:S(2)}) async-start(), calls=%async_computation.11 | async-start | bytes 2064384 | tf_op jit(solution)/shard_map/all_gather | solution.py:67
  394.1 81.8 %all-gather.19.cloned.1.call-start = ((), (), s32[]{:S(2)}) async-start(), calls=%async_computation.12 | async-start | bytes 2064384 | tf_op jit(solution)/shard_map/all_gather | solution.py:68
  394.8 168.2 %reduce-scatter.11.cloned.1.call-start = ((), (), s32[]{:S(2)}) async-start(), calls=%async_computation.13 | async-start | bytes 2228224 | tf_op jit(solution)/shard_map/reduce_scatter | solution.py:70
  482.9 95.2 %copy-start.2 = (bf16[64,1024]{1,0:T(8,128)(2,1)S(1)}, bf16[64,1024]{1,0:T(8,128)(2,1)}, u32[]{:S(2)}) copy-start(bf16[64,1024]{1,0:T(8,128)(2,1)} %broadcast_select_fusion) | copy-start | bytes 393220
  482.9 120.5 %all-gather.23.cloned.1.call-start = ((), (), s32[]{:S(2)}) async-start(), calls=%async_computation.15 | async-start | bytes 2064384 | tf_op jit(solution)/shard_map/all_gather | solution.py:93
  483.6 174.0 %all-gather.21.cloned.1.call-start = ((), (), s32[]{:S(2)}) async-start(), calls=%async_computation.14 | async-start | bytes 2228224 | tf_op jit(solution)/shard_map/all_gather | solution.py:96
  657.6 5.9 copy-start.7
  657.6 5.9 copy-start.8
Sparse Core Ops, SparseCore 0:
  10.4 52.8 all-gather.8
  69.3 37.5 reduce-scatter.4
  109.2 39.4 all-gather.10
  151.0 39.1 all-gather.12
  197.4 80.0 reduce-scatter.6
  303.1 45.4 all-gather.14
  354.5 37.4 reduce-scatter.8
  394.5 39.5 all-gather.16
  436.6 39.1 all-gather.18
  483.0 79.9 reduce-scatter.10
  565.4 37.9 all-gather.22
  606.3 51.2 all-gather.20
where the time goes:
time: 674 us
  waiting for transfers between devices  528 us (78%)
  blocking collectives  61.3 us (9%)
  matrix products  52.1 us (8%)
  between operations  14.3 us (2%)
  other arithmetic  9.71 us (1%)
  starting transfers between devices  8.49 us (1%)
    reduce_scatter x2, waiting for transfers between devices, backward_data(): lax.psum_scatter((contract_cols(gate_grads, gate_w) + contract_cols(up_gr...  160 us
    all_gather x2, waiting for transfers between devices, backward_data(): cot_full = lax.all_gather(cotangent, 'col', axis=0, tiled=True)  101 us
    all_gather x2, waiting for transfers between devices, backward_data(): lax.all_gather(gate_grad, 'row', axis=0, tiled=True)  78.6 us
    reduce_scatter x2, waiting for transfers between devices, backward_data(): lax.psum_scatter(contract_cols(cot_full, down_w).astype(jnp.bfloat16), 'r...  75.3 us
    all_gather x2, waiting for transfers between devices, backward_data(): lax.all_gather(up_grad, 'row', axis=0, tiled=True)  71.5 us
    dot_general x6, matrix products, contract_cols(): lax.dot_general(left, right, (((1,), (1,)), ((), ())), preferred_element_...  37.1 us
    psum x1, blocking collectives, body(): lax.psum(jnp.sum(normed_grad * hidden_f * inv_rms[:, None], axis=0), 'col')  33.7 us
    psum x2, blocking collectives, backward_data(): cross = lax.psum(cross, 'row')  27.6 us
  transfers between devices with their start and end apart: 13, of which 13 were waited for; matrix products, arithmetic and copies ran while one was open for 3% of the time, Pallas kernels for 0%

commit v1 on v0

v1 whole, which is shorter than its diff:
```python
import jax
import jax.numpy as jnp
from jax import lax
from jax.experimental import pallas as pl
from jax.experimental.pallas import tpu as pltpu
from jax.sharding import PartitionSpec as P

D = 8192
EPSILON = 1e-05

bf16 = jnp.bfloat16
f32 = jnp.float32


def dot(left, right, dims):
    return lax.dot_general(left, right, (dims, ((), ())), preferred_element_type=f32)


def swap(block):
    return lax.ppermute(block, "section", [(0, 1), (1, 0)])


def after(block, event):
    return lax.optimization_barrier((block, event))[0]


def exchange(blocks, axis):
    return lax.all_to_all(blocks, axis, 0, 0)


def spread(block, axis):
    copies = jnp.broadcast_to(block[None], (lax.axis_size(axis),) + block.shape)
    return exchange(copies, axis)


def unit_kernel(hidden_grad, saved, gate_w, up_w, gate_out, up_out, partial):
    grad_f = hidden_grad[...].astype(f32)
    gate_f, up_f = saved[0].astype(f32), saved[1].astype(f32)
    sig = jax.nn.sigmoid(gate_f)
    gate_grad = (grad_f * up_f * sig * (1.0 + gate_f * (1.0 - sig))).astype(bf16)
    up_grad = (grad_f * gate_f * sig).astype(bf16)
    gate_out[...] = gate_grad
    up_out[...] = up_grad
    total = dot(gate_grad, gate_w[...], ((1,), (1,))) + dot(up_grad, up_w[...], ((1,), (1,)))
    partial[...] = total.astype(bf16)


def unit_grads(hidden_grad, saved, gate_w, up_w):
    tokens, units = hidden_grad.shape
    features = gate_w.shape[0]
    tile = 128
    by_tokens = pl.BlockSpec((tile, units), lambda i: (i, 0))
    whole = pl.BlockSpec((features, units), lambda i: (0, 0))
    return pl.pallas_call(
        unit_kernel,
        grid=(tokens // tile,),
        in_specs=[by_tokens, pl.BlockSpec((2, tile, units), lambda i: (0, i, 0)), whole, whole],
        out_specs=[by_tokens, by_tokens, pl.BlockSpec((tile, features), lambda i: (i, 0))],
        out_shape=[
            jax.ShapeDtypeStruct((tokens, units), bf16),
            jax.ShapeDtypeStruct((tokens, units), bf16),
            jax.ShapeDtypeStruct((tokens, features), bf16),
        ],
        compiler_params=pltpu.CompilerParams(vmem_limit_bytes=40 * 1024 * 1024),
        cost_estimate=pl.CostEstimate(
            flops=4 * tokens * units * features,
            bytes_accessed=10 * tokens * units + 4 * units * features + 2 * tokens * features,
            transcendentals=tokens * units,
        ),
    )(hidden_grad, saved, gate_w, up_w)


def body(hidden_in, norm_gain, gate_saved, up_saved, w_gate, w_up, w_down, out_grad):
    rows, cols = lax.axis_size("row"), lax.axis_size("col")
    first = lax.axis_index("section") == 0
    features = hidden_in.shape[2]
    units = gate_saved.shape[2]
    half = hidden_in.shape[1] // 2

    def mine_theirs(block):
        low, high = block[:half], block[half:]
        return jnp.where(first, low, high), jnp.where(first, high, low)

    def by_layer(own, other):
        return jnp.where(first, other, own), jnp.where(first, own, other)

    gate_blocks = gate_saved[0].reshape(2, 2, half, units)
    up_blocks = up_saved[0].reshape(2, 2, half, units)
    saved = jnp.stack([gate_blocks, up_blocks])
    saved_low, saved_high = saved[:, :, 0], saved[:, :, 1]
    saved_mine = jnp.where(first, saved_low, saved_high)
    saved_other = swap(jnp.where(first, saved_high, saved_low))

    def gather_saved(block):
        block = block.reshape(2, 1, 2 * half, units)
        return lax.all_gather(block, "row", axis=2, tiled=True)

    saved1, saved0 = by_layer(saved_mine, saved_other)
    down1, down0 = by_layer(w_down[0], swap(after(w_down[0], saved_other)))
    down1, down0 = after((down1, down0), saved1)
    hid_mine, hid_theirs = mine_theirs(hidden_in[0])
    hid_other = swap(hid_theirs)
    gain1, gain0 = by_layer(norm_gain[0], swap(norm_gain[0]))
    hid1, hid0 = by_layer(hid_mine, hid_other)

    def scatter_units(cot, down_w):
        cot_all = spread(cot, "col").reshape(cols * half, features)
        return cot_all, dot(cot_all, down_w, ((1,), (1,))).astype(bf16)

    def gather_units(partial):
        pieces = exchange(partial.reshape(rows, 2 * half, units), "row")
        return jnp.sum(pieces.astype(f32), axis=0).astype(bf16)

    def all_units(grad_local):
        return spread(grad_local, "row").reshape(cols * half, units)

    def normed_grads(partial):
        pieces = exchange(partial.reshape(cols, half, features), "col")
        return jnp.sum(pieces.astype(f32), axis=0)

    def inner(normed_grad, hidden, gain):
        return jnp.sum(gain * normed_grad * hidden.astype(f32), axis=1)

    def over_rows(sums):
        return jnp.sum(spread(sums.reshape(1, -1), "row"), axis=0)[0]

    def finish(cot, normed_grad, hidden, inv_rms, gain, cross):
        return (
            cot.astype(f32)
            + inv_rms[:, None] * gain * normed_grad
            - hidden.astype(f32) * (inv_rms**3 * cross / D)[:, None]
        ).astype(bf16)

    def gain_part(normed_grad, hidden, inv_rms):
        return jnp.sum(normed_grad * hidden.astype(f32) * inv_rms[:, None], axis=0)

    def activation(saved):
        gate_f = saved[0].astype(f32)
        return (gate_f * jax.nn.sigmoid(gate_f) * saved[1].astype(f32)).astype(bf16)

    def both_halves(layer1, layer0, event):
        layer1, layer0, _ = lax.optimization_barrier((layer1, layer0, event))
        own = jnp.where(first, layer0, layer1)
        other = swap(jnp.where(first, layer1, layer0))
        return jnp.concatenate([own, other], axis=0)

    def handed(block, source, target):
        return lax.ppermute(block, "section", [(source, target)])

    def joined_halves(own1, other1, own0, other0):
        return jnp.concatenate([jnp.where(first, own0, own1), jnp.where(first, other0, other1)], axis=0)

    saved1 = gather_saved(saved1)
    cot1 = mine_theirs(out_grad)[0]
    cot_all1, partial = scatter_units(cot1, down1)
    gate_own, up_own = w_gate[0], w_up[0]
    gate_swapped = swap(after(gate_own, cot_all1))
    up_swapped = swap(after(up_own, cot_all1))
    grad_local = gather_units(partial)
    gates1, gates0 = lax.optimization_barrier(by_layer(gate_own, gate_swapped))
    ups1, ups0 = lax.optimization_barrier(by_layer(up_own, up_swapped))
    both = jnp.concatenate([hid_mine, hid_theirs, hid_other], axis=0).astype(f32)
    squares = after(jnp.sum(both * both, axis=1), grad_local)

    grad_local = after(grad_local, saved1)
    gate_grad1, up_grad1, partial = unit_grads(all_units(grad_local), saved1[:, 0], gates1, ups1)
    saved0 = gather_saved(after(saved0, gate_grad1))
    normed_grad1 = normed_grads(partial)
    sums = over_rows(jnp.concatenate([squares, inner(normed_grad1, hid1, gain1)]))
    inv = lax.rsqrt(sums[: 3 * half] / D + EPSILON)
    inv1, inv0 = by_layer(inv[:half], inv[2 * half :])
    result1 = finish(cot1, normed_grad1, hid1, inv1, gain1, sums[3 * half :])

    cot_all0, partial = scatter_units(result1, down0)
    partial = after(partial, saved0)
    normed = jnp.concatenate([hid_mine, hid_theirs], axis=0).astype(f32)
    normed = normed * inv[: 2 * half, None] * norm_gain[0]
    normed = after(normed.astype(bf16).reshape(2, half, features), cot_all0)
    normed = lax.all_gather(normed, "col", axis=1, tiled=True)
    grad_local = gather_units(partial)
    hidden_grad = all_units(grad_local)
    gate_from_other = handed(after(gate_grad1, cot_all0), 0, 1)
    up_from_other = handed(after(up_grad1, cot_all0), 0, 1)
    cot_both = both_halves(cot_all1, cot_all0, cot_all0)
    act_both = both_halves(activation(saved1[:, 0]), activation(saved0[:, 0]), cot_all0)
    grad_down = dot(act_both, cot_both, ((0,), (0,))).astype(bf16)
    hidden_grad = after(hidden_grad, grad_down)
    gate_grad0, up_grad0, partial = unit_grads(hidden_grad, saved0[:, 0], gates0, ups0)
    partial = after(partial, normed)
    gate_grads = joined_halves(gate_grad1, gate_from_other, gate_grad0, handed(gate_grad0, 1, 0))
    up_grads = joined_halves(up_grad1, up_from_other, up_grad0, handed(up_grad0, 1, 0))
    normed_grad0 = normed_grads(partial)
    cross = over_rows(inner(normed_grad0, hid0, gain0))
    result0 = finish(result1, normed_grad0, hid0, inv0, gain0, cross)

    tokens = 2 * half * cols
    normed = normed.reshape(tokens, features)
    grad_gate = dot(normed, gate_grads, ((0,), (0,))).astype(bf16)
    grad_up = dot(normed, up_grads, ((0,), (0,))).astype(bf16)

    gain1_part = gain_part(normed_grad1, hid1, inv1)
    gain0_part = gain_part(normed_grad0, hid0, inv0)
    gain_parts = jnp.stack([jnp.where(first, gain0_part, gain1_part), jnp.where(first, gain1_part, gain0_part)])
    gain_parts = jnp.sum(spread(gain_parts, "col"), axis=0)
    gain_total = gain_parts[0] + swap(gain_parts[1])
    own = jnp.where(first, result0, result1)
    other = swap(jnp.where(first, result1, result0))
    result = jnp.where(first, jnp.concatenate([own, other]), jnp.concatenate([other, own]))
    return (result[None], gain_total[None], grad_gate[None], grad_up[None], grad_down[None])


def solution(mesh):
    placed = (
        P("section", "col", "row"),
        P("section", "row"),
        P("section", "row", "col"),
        P("section", "row", "col"),
        P("section", "row", "col"),
        P("section", "row", "col"),
        P("section", "col", "row"),
        P("col", "row"),
    )
    return jax.shard_map(
        body,
        mesh=mesh,
        in_specs=placed,
        out_specs=(
            P("section", "col", "row"),
            P("section", "row"),
            P("section", "row", "col"),
            P("section", "row", "col"),
            P("section", "col", "row"),
        ),
        check_vma=False,
    )
```

time: 674 us -> 306 us (0.45)
  waiting for transfers between devices: 528 us -> 128 us
  starting transfers between devices: 8.49 us -> 80.6 us
  blocking collectives: 61.3 us -> 9.45 us
  matrix products: 52.1 us -> 20.2 us
  other arithmetic: 9.71 us -> 26 us
  local copies, waits for them, and re-layouts: 0.04 us -> 13.8 us
  Pallas kernels: 0 us -> 12.3 us
    all_gather x8 -> x3, waiting for transfers between devices: 290 us -> 0.02 us  [the longest x2 0.02 us: gather_saved(): return lax.all_gather(block, 'row', axis=2, tiled=True)]
    reduce_scatter x4 -> x0, waiting for transfers between devices: 235 us -> none  [the longest x2 160 us: backward_data(): lax.psum_scatter((contract_cols(gate_grads, gate_w) + contract_cols(up_gr...]
    all_to_all x0 -> x10, waiting for transfers between devices: none -> 124 us  [exchange(): return lax.all_to_all(blocks, axis, 0, 0)]
    psum x3 -> x0, blocking collectives: 61.3 us -> none  [the longest x1 33.7 us: body(): lax.psum(jnp.sum(normed_grad * hidden_f * inv_rms[:, None], axis=0), 'col')]
    all_to_all x0 -> x10, starting transfers between devices: none -> 46.6 us  [exchange(): return lax.all_to_all(blocks, axis, 0, 0)]
    dot_general x9 -> x5, matrix products: 52.1 us -> 20.2 us  [dot(): lax.dot_general(left, right, (dims, ((), ())), preferred_element_type=f32)]
    ppermute x1 -> x14, starting transfers between devices: 8.01 us -> 33.8 us  [the longest x10 21.1 us: swap(): return lax.ppermute(block, 'section', [(0, 1), (1, 0)])]
    select_n x1 -> x16, other arithmetic: 0.67 us -> 19.7 us  [the longest x5 12.2 us: by_layer(): return (jnp.where(first, other, own), jnp.where(first, own, other))]
  transfers between devices with their start and end apart: 13 -> 27, of which waited for: 13 -> 14; matrix products, arithmetic and copies ran while one was open for 3% -> 16% of each run, Pallas kernels for 0% -> 2%
where the time goes in v1:
time: 306 us; the launch traced here: 304 us
  waiting for transfers between devices  128 us (42%)
  starting transfers between devices  80.6 us (26%)
  other arithmetic  26 us (8%)
  matrix products  20.2 us (7%)
  between operations  14.1 us (5%)
  local copies, waits for them, and re-layouts  13.8 us (5%)
  Pallas kernels  12.3 us (4%)
  blocking collectives  9.45 us (3%)
    all_to_all x10, waiting for transfers between devices, exchange(): return lax.all_to_all(blocks, axis, 0, 0)  124 us
    all_to_all x10, starting transfers between devices, exchange(): return lax.all_to_all(blocks, axis, 0, 0)  46.6 us
    ppermute x10, starting transfers between devices, swap(): return lax.ppermute(block, 'section', [(0, 1), (1, 0)])  21.1 us
    dot_general x5, matrix products, dot(): lax.dot_general(left, right, (dims, ((), ())), preferred_element_type=f32)  20.2 us
    ppermute x4, starting transfers between devices, handed(): return lax.ppermute(block, 'section', [(source, target)])  12.7 us
    pallas_call x2, Pallas kernels, unit_grads(): pl.pallas_call(unit_kernel, grid=(tokens // tile,), in_specs=[by_tokens,...  12.3 us
    select_n x5, other arithmetic, by_layer(): return (jnp.where(first, other, own), jnp.where(first, own, other))  12.2 us
    all_to_all x1, blocking collectives, exchange(): return lax.all_to_all(blocks, axis, 0, 0)  9.45 us
  transfers between devices with their start and end apart: 27, of which 14 were waited for; matrix products, arithmetic and copies ran while one was open for 16% of the time, Pallas kernels for 2%

profile of v1, /device:TPU:1, one launch (start us, length us, event | category | flops | bytes accessed | tf_op | source)
XLA Modules:
  0.0 304.2 jit_solution(4978550062873593398)
XLA Ops:
  7.2 1.1 select_bitcast_fusion
  8.3 3.3 %collective-permute-start.1 = (bf16[2,2,32,896]{3,2,1,0:T(8,128)(2,1)S(1)}, bf16[2,2,32,896]{3,2,1,0:T(8,128)(2,1)S(1)}, u32[]{:S(2)}, u32[]{:S(2)}) collective-permute-start(bf16[2,2,32,896]{3,2,1,0:T(8,128)(2,1)S(1)} %select_bitcast_fusion), channel_id=1, source_target_pairs={{0,128},{128,0},{1,129},{129,1},{2,130},{130,2},{3,131},{131,3},{4... | collective-permute-start | bytes 688136 | tf_op jit(solution)/shard_map/ppermute | solution.py:20
  11.7 1.1 collective-permute-done.1
  13.2 2.0 bitcast_select_fusion
  15.3 1.1 broadcast_in_dim.22
  16.4 5.0 %all-to-all-start = ((bf16[16,32,1024]{2,1,0:T(8,128)(2,1)}), bf16[16,32,1024]{2,1,0:T(8,128)(2,1)S(1)}, u32[]{:S(2)}, u32[]{:S(2)}) async-start(bf16[16,32,1024]{2,1,0:T(8,128)(2,1)} %broadcast_in_dim.22), calls=%async_computation | async-start | bytes 2097152 | tf_op jit(solution)/shard_map/all_to_all | solution.py:28
  21.4 3.6 %broadcast_select_fusion.4 = (bf16[896,1024]{1,0:T(8,128)(2,1)}, bf16[896,1024]{1,0:T(8,128)(2,1)}) fusion(bf16[896,1024]{1,0:T(8,128)(2,1)} %collective-permute-done.2, pred[]{:T(512)S(6)} %eq.3, bf16[1,896,1024]{2,1,0:T(8,128)(2,1)S(1)} %copy-done.12), kind=kLoop, calls=%fused_computation.37 | loop fusion | flops 1835008 | bytes 7340033 | tf_op jit(solution)/shard_map/jit(_where)/select_n | solution.py:85
  25.0 13.2 %all-to-all-done = bf16[16,32,1024]{2,1,0:T(8,128)(2,1)S(1)} async-done(((bf16[16,32,1024]{2,1,0:T(8,128)(2,1)}), bf16[16,32,1024]{2,1,0:T(8,128)(2,1)S(1)}, u32[]{:S(2)}, u32[]{:S(2)}) %all-to-all-start) | async-done | bytes 1048608 | tf_op jit(solution)/shard_map/all_to_all | solution.py:28
  38.1 4.1 %convolution_convert_fusion.1 = bf16[512,896]{1,0:T(8,128)(2,1)} fusion(bf16[512,1024]{1,0:T(8,128)(2,1)S(1)} %bitcast.112, bf16[896,1024]{1,0:T(8,128)(2,1)} %get-tuple-element.34), kind=kOutput, calls=%fused_computation.41 | convolution fusion | flops 939982848 | bytes 3801088 | tf_op jit(solution)/shard_map/dot_general | solution.py:16
  42.2 8.2 %all-to-all-start.1 = ((bf16[8,64,896]{2,1,0:T(8,128)(2,1)}), bf16[8,64,896]{2,1,0:T(8,128)(2,1)S(1)}, u32[]{:S(2)}, u32[]{:S(2)}) async-start(bf16[8,64,896]{2,1,0:T(8,128)(2,1)} %bitcast.8), calls=%async_computation.1 | async-start | bytes 1835008 | tf_op jit(solution)/shard_map/all_to_all | solution.py:28
  50.4 2.2 collective-permute-start.4
  52.7 22.2 %all-to-all-done.1 = bf16[8,64,896]{2,1,0:T(8,128)(2,1)S(1)} async-done(((bf16[8,64,896]{2,1,0:T(8,128)(2,1)}), bf16[8,64,896]{2,1,0:T(8,128)(2,1)S(1)}, u32[]{:S(2)}, u32[]{:S(2)}) %all-to-all-start.1) | async-done | bytes 917536 | tf_op jit(solution)/shard_map/all_to_all | solution.py:28
  75.1 1.0 broadcast_in_dim.23
  76.1 3.7 %all-to-all-start.2 = ((bf16[8,64,896]{2,1,0:T(8,128)(2,1)}), bf16[8,64,896]{2,1,0:T(8,128)(2,1)S(1)}, u32[]{:S(2)}, u32[]{:S(2)}) async-start(bf16[8,64,896]{2,1,0:T(8,128)(2,1)} %broadcast_in_dim.23), calls=%async_computation.2 | async-start | bytes 1835008 | tf_op jit(solution)/shard_map/all_to_all | solution.py:28
  79.9 6.6 %broadcast_select_fusion = (bf16[1024,896]{1,0:T(8,128)(2,1)}, bf16[1024,896]{1,0:T(8,128)(2,1)}, bf16[1024,896]{1,0:T(8,128)(2,1)}, bf16[1024,896]{1,0:T(8,128)(2,1)}) fusion(bf16[1024,896]{1,0:T(8,128)(2,1)} %collective-permute-done.5, pred[]{:T(512)S(6)} %eq.3, bf16[1,1024,896]{2,1,0:T(8,128)(2,1)} %param.13, ...), kind=kLoop, calls=%fused_computation.33 | loop fusion | flops 3670016 | bytes 14680065 | tf_op jit(solution)/shard_map/jit(_where)/select_n | solution.py:85
  86.4 19.8 %all-to-all-done.2 = bf16[8,64,896]{2,1,0:T(8,128)(2,1)S(1)} async-done(((bf16[8,64,896]{2,1,0:T(8,128)(2,1)}), bf16[8,64,896]{2,1,0:T(8,128)(2,1)S(1)}, u32[]{:S(2)}, u32[]{:S(2)}) %all-to-all-start.2) | async-done | bytes 917536 | tf_op jit(solution)/shard_map/all_to_all | solution.py:28
  106.2 1.5 copy-done.5
  107.7 1.5 copy-done.6
  109.2 6.2 %shard_map.119 = (bf16[512,896]{1,0:T(8,128)(2,1)}, bf16[512,896]{1,0:T(8,128)(2,1)}, bf16[512,1024]{1,0:T(8,128)(2,1)}) custom-call(bf16[512,896]{1,0:T(8,128)(2,1)S(1)} %bitcast.111, bf16[2,512,896]{2,1,0:T(8,128)(2,1)S(1)} %bitcast.107, bf16[1024,896]{1,0:T(8,128)(2,1)S(1)} %copy-done.6, bf16[1024,896]{1,0:T(8,128)(2,1)S(1)} %copy-done.5), custom_call_target="tpu_custom_call" | custom-call | flops 1879048192 | bytes 9306112 | tf_op jit(solution)/shard_map/pallas_call | solution.py:54
  115.4 6.0 %all-to-all-start.3 = ((bf16[16,32,1024]{2,1,0:T(8,128)(2,1)}), bf16[16,32,1024]{2,1,0:T(8,128)(2,1)S(1)}, u32[]{:S(2)}, u32[]{:S(2)}) async-start(bf16[16,32,1024]{2,1,0:T(8,128)(2,1)} %bitcast.15), calls=%async_computation.3 | async-start | bytes 2097152 | tf_op jit(solution)/shard_map/all_to_all | solution.py:28
  121.5 0.7 all-gather.6.cloned.1.call-update
  122.2 1.8 collective-permute-start.3
  124.2 0.7 collective-permute-done.3
  124.9 11.9 %all-to-all-done.3 = bf16[16,32,1024]{2,1,0:T(8,128)(2,1)S(1)} async-done(((bf16[16,32,1024]{2,1,0:T(8,128)(2,1)}), bf16[16,32,1024]{2,1,0:T(8,128)(2,1)S(1)}, u32[]{:S(2)}, u32[]{:S(2)}) %all-to-all-start.3) | async-done | bytes 1048608 | tf_op jit(solution)/shard_map/all_to_all | solution.py:28
  137.3 9.4 %all_to_all.55 = f32[8,1,128]{2,1,0:T(1,128)S(1)} all-to-all(f32[8,1,128]{2,1,0:T(1,128)S(1)} %broadcast_in_dim.24), channel_id=1, replica_groups=mesh['section'=2,'row'=8,'col'=16] {'row'}, dimensions={0} | all-to-all | bytes 8192 | tf_op jit(solution)/shard_map/all_to_all | solution.py:28
  147.0 1.1 broadcast_in_dim.25
  148.1 4.5 %all-to-all-start.5 = ((bf16[16,32,1024]{2,1,0:T(8,128)(2,1)}), bf16[16,32,1024]{2,1,0:T(8,128)(2,1)S(1)}, u32[]{:S(2)}, u32[]{:S(2)}) async-start(bf16[16,32,1024]{2,1,0:T(8,128)(2,1)} %broadcast_in_dim.25), calls=%async_computation.5 | async-start | bytes 2097152 | tf_op jit(solution)/shard_map/all_to_all | solution.py:28
  152.7 14.1 %all-to-all-done.5 = bf16[16,32,1024]{2,1,0:T(8,128)(2,1)S(1)} async-done(((bf16[16,32,1024]{2,1,0:T(8,128)(2,1)}), bf16[16,32,1024]{2,1,0:T(8,128)(2,1)S(1)}, u32[]{:S(2)}, u32[]{:S(2)}) %all-to-all-start.5) | async-done | bytes 1048608 | tf_op jit(solution)/shard_map/all_to_all | solution.py:28
  166.8 4.1 %convolution_convert_fusion = bf16[512,896]{1,0:T(8,128)(2,1)} fusion(bf16[512,1024]{1,0:T(8,128)(2,1)S(1)} %bitcast.114, bf16[896,1024]{1,0:T(8,128)(2,1)} %get-tuple-element.42), kind=kOutput, calls=%fused_computation.40 | convolution fusion | flops 939982848 | bytes 3801088 | tf_op jit(solution)/shard_map/dot_general | solution.py:16
  170.9 4.2 %all-to-all-start.6 = ((bf16[8,64,896]{2,1,0:T(8,128)(2,1)}), bf16[8,64,896]{2,1,0:T(8,128)(2,1)}, u32[]{:S(2)}, u32[]{:S(2)}) async-start(bf16[8,64,896]{2,1,0:T(8,128)(2,1)} %bitcast.117), calls=%async_computation.6 | async-start | bytes 1835008 | tf_op jit(solution)/shard_map/all_to_all | solution.py:28
  175.2 0.8 fusion.35
  176.0 1.5 fusion.24
  177.5 1.5 broadcast_select_fusion.7
  178.9 4.3 %collective-permute-start.7 = (bf16[512,1024]{1,0:T(8,128)(2,1)}, bf16[512,1024]{1,0:T(8,128)(2,1)}, u32[]{:S(2)}, u32[]{:S(2)}) collective-permute-start(bf16[512,1024]{1,0:T(8,128)(2,1)} %get-tuple-element.76), channel_id=1, source_target_pairs={{0,128},{128,0},{1,129},{129,1},{2,130},{130,2},{3,131},{131,3},{4... | collective-permute-start | bytes 3145736 | tf_op jit(solution)/shard_map/ppermute | solution.py:20
  183.3 14.5 %all-to-all-done.6 = bf16[8,64,896]{2,1,0:T(8,128)(2,1)} async-done(((bf16[8,64,896]{2,1,0:T(8,128)(2,1)}), bf16[8,64,896]{2,1,0:T(8,128)(2,1)}, u32[]{:S(2)}, u32[]{:S(2)}) %all-to-all-start.6) | async-done | bytes 917536 | tf_op jit(solution)/shard_map/all_to_all | solution.py:28
  197.8 1.3 reduce_sum.122
  199.1 1.1 broadcast_in_dim.26
  200.2 3.7 %all-to-all-start.7 = ((bf16[8,64,896]{2,1,0:T(8,128)(2,1)}), bf16[8,64,896]{2,1,0:T(8,128)(2,1)S(1)}, u32[]{:S(2)}, u32[]{:S(2)}) async-start(bf16[8,64,896]{2,1,0:T(8,128)(2,1)} %broadcast_in_dim.26), calls=%async_computation.7 | async-start | bytes 1835008 | tf_op jit(solution)/shard_map/all_to_all | solution.py:28
  205.3 4.3 %collective-permute-start.6 = (bf16[512,896]{1,0:T(8,128)(2,1)S(1)}, bf16[512,896]{1,0:T(8,128)(2,1)S(1)}, u32[]{:S(2)}, u32[]{:S(2)}) collective-permute-start(bf16[512,896]{1,0:T(8,128)(2,1)S(1)} %get-tuple-element.78), channel_id=1, source_target_pairs={{0,128},{128,0},{1,129},{129,1},{2,130},{130,2},{3,131},{131,3},{4... | collective-permute-start | bytes 2752520 | tf_op jit(solution)/shard_map/ppermute | solution.py:20
  209.6 1.3 collective-permute-start.13
  210.9 0.8 collective-permute-done.6
  211.7 4.7 %fusion.29 = bf16[896,1024]{1,0:T(8,128)(2,1)} fusion(bf16[512,1024]{1,0:T(8,128)(2,1)} %collective-permute-done.7, bf16[512,1024]{1,0:T(8,128)(2,1)S(1)} %copy-done.13, bf16[512,896]{1,0:T(8,128)(2,1)S(1)} %collective-permute-done.6, bf16[512,896]{1,0:T(8,128)(2,1)S(1)} %get-tuple-element.77), kind=kOutput, calls=%fused_computation.39 | convolution fusion | flops 1887830016 | bytes 5767168 | tf_op jit(solution)/shard_map/dot_general | solution.py:16
  216.4 10.1 %all-to-all-done.7 = bf16[8,64,896]{2,1,0:T(8,128)(2,1)S(1)} async-done(((bf16[8,64,896]{2,1,0:T(8,128)(2,1)}), bf16[8,64,896]{2,1,0:T(8,128)(2,1)S(1)}, u32[]{:S(2)}, u32[]{:S(2)}) %all-to-all-start.7) | async-done | bytes 917536 | tf_op jit(solution)/shard_map/all_to_all | solution.py:28
  226.5 1.5 copy-done.2
  228.0 1.5 copy-done.4
  229.5 6.2 %shard_map.120 = (bf16[512,896]{1,0:T(8,128)(2,1)}, bf16[512,896]{1,0:T(8,128)(2,1)}, bf16[512,1024]{1,0:T(8,128)(2,1)}) custom-call(bf16[512,896]{1,0:T(8,128)(2,1)S(1)} %bitcast.110, bf16[2,512,896]{2,1,0:T(8,128)(2,1)S(1)} %bitcast.109, bf16[1024,896]{1,0:T(8,128)(2,1)S(1)} %copy-done.2, bf16[1024,896]{1,0:T(8,128)(2,1)S(1)} %copy-done.1), custom_call_target="tpu_custom_call" | custom-call | flops 1879048192 | bytes 9306112 | tf_op jit(solution)/shard_map/pallas_call | solution.py:54
  235.7 7.0 %collective-permute-start.12 = (bf16[512,896]{1,0:T(8,128)(2,1)}, bf16[512,896]{1,0:T(8,128)(2,1)}, u32[]{:S(2)}, u32[]{:S(2)}) collective-permute-start(bf16[512,896]{1,0:T(8,128)(2,1)} %get-tuple-element.58), channel_id=1, source_target_pairs={{128,0},{129,1},{130,2},{131,3},{132,4},{133,5},{134,6},{135,7},{1... | collective-permute-start | bytes 2752520 | tf_op jit(solution)/shard_map/ppermute | solution.py:148
  242.7 1.3 collective-permute-start.11
  244.0 3.1 %collective-permute-start.10 = (bf16[512,896]{1,0:T(8,128)(2,1)}, bf16[512,896]{1,0:T(8,128)(2,1)S(1)}, u32[]{:S(2)}, u32[]{:S(2)}) collective-permute-start(bf16[512,896]{1,0:T(8,128)(2,1)} %get-tuple-element.56), channel_id=1, source_target_pairs={{128,0},{129,1},{130,2},{131,3},{132,4},{133,5},{134,6},{135,7},{1... | collective-permute-start | bytes 2752520 | tf_op jit(solution)/shard_map/ppermute | solution.py:148
  247.3 4.4 %all-to-all-start.8 = ((bf16[16,32,1024]{2,1,0:T(8,128)(2,1)}), bf16[16,32,1024]{2,1,0:T(8,128)(2,1)S(1)}, u32[]{:S(2)}, u32[]{:S(2)}) async-start(bf16[16,32,1024]{2,1,0:T(8,128)(2,1)} %bitcast.34), calls=%async_computation.8 | async-start | bytes 2097152 | tf_op jit(solution)/shard_map/all_to_all | solution.py:28
  251.7 1.3 broadcast_select_fusion.9
  253.0 1.3 broadcast_select_fusion.11
  254.3 1.3 broadcast_select_fusion.8
  255.7 1.5 copy-done.17
  257.2 3.6 %convert_bitcast_fusion = bf16[1,1024,896]{2,1,0:T(8,128)(2,1)} fusion(bf16[1024,1024]{1,0:T(8,128)(2,1)S(1)} %bitcast.138, bf16[512,896]{1,0:T(8,128)(2,1)S(1)} %broadcast_select_fusion.8, bf16[512,896]{1,0:T(8,128)(2,1)S(1)} %broadcast_select_fusion.9), kind=kOutput, calls=%fused_computation.29 | convolution fusion | flops 1883635712 | bytes 5767168 | tf_op jit(solution)/shard_map/dot_general | solution.py:16
  260.8 3.6 %convert_bitcast_fusion.1 = bf16[1,1024,896]{2,1,0:T(8,128)(2,1)} fusion(bf16[1024,1024]{1,0:T(8,128)(2,1)S(1)} %bitcast.139, bf16[512,896]{1,0:T(8,128)(2,1)S(1)} %broadcast_select_fusion.10, bf16[512,896]{1,0:T(8,128)(2,1)S(1)} %broadcast_select_fusion.11), kind=kOutput, calls=%fused_computation.30 | convolution fusion | flops 1883635712 | bytes 5767168 | tf_op jit(solution)/shard_map/dot_general | solution.py:16
  264.5 7.2 %all-to-all-done.8 = bf16[16,32,1024]{2,1,0:T(8,128)(2,1)S(1)} async-done(((bf16[16,32,1024]{2,1,0:T(8,128)(2,1)}), bf16[16,32,1024]{2,1,0:T(8,128)(2,1)S(1)}, u32[]{:S(2)}, u32[]{:S(2)}) %all-to-all-start.8) | async-done | bytes 1048608 | tf_op jit(solution)/shard_map/all_to_all | solution.py:28
  272.7 3.3 %all-to-all-start.9 = ((f32[8,1,32]{2,1,0:T(1,128)}), f32[8,1,32]{2,1,0:T(1,128)S(1)}, u32[]{:S(2)}, u32[]{:S(2)}) async-start(f32[8,1,32]{2,1,0:T(1,128)} %broadcast_in_dim.27), calls=%async_computation.9 | async-start | bytes 8192 | tf_op jit(solution)/shard_map/all_to_all | solution.py:28
  276.0 6.3 %all-to-all-done.9 = f32[8,1,32]{2,1,0:T(1,128)S(1)} async-done(((f32[8,1,32]{2,1,0:T(1,128)}), f32[8,1,32]{2,1,0:T(1,128)S(1)}, u32[]{:S(2)}, u32[]{:S(2)}) %all-to-all-start.9) | async-done | bytes 1056 | tf_op jit(solution)/shard_map/all_to_all | solution.py:28
  282.4 0.7 broadcast_in_dim.28
  283.1 3.5 %all-to-all-start.10 = ((f32[16,2,1024]{2,1,0:T(2,128)}), f32[16,2,1024]{2,1,0:T(2,128)S(1)}, u32[]{:S(2)}, u32[]{:S(2)}) async-start(f32[16,2,1024]{2,1,0:T(2,128)} %broadcast_in_dim.28), calls=%async_computation.10 | async-start | bytes 262144 | tf_op jit(solution)/shard_map/all_to_all | solution.py:28
  286.8 1.7 collective-permute-start.8
  288.5 4.9 %all-to-all-done.10 = f32[16,2,1024]{2,1,0:T(2,128)S(1)} async-done(((f32[16,2,1024]{2,1,0:T(2,128)}), f32[16,2,1024]{2,1,0:T(2,128)S(1)}, u32[]{:S(2)}, u32[]{:S(2)}) %all-to-all-start.10) | async-done | bytes 131104 | tf_op jit(solution)/shard_map/all_to_all | solution.py:28
  293.4 2.9 collective-permute-start.9
  (85 shorter events, 6.0 us)
Async XLA Ops:
  7.2 8.1 %copy-start.15 = (bf16[64,1024]{1,0:T(8,128)(2,1)S(1)}, bf16[64,1024]{1,0:T(8,128)(2,1)}, u32[]{:S(2)}) copy-start(bf16[64,1024]{1,0:T(8,128)(2,1)} %param.15) | copy-start | bytes 393220
  7.2 67.9 %all-gather.4.cloned.1.call-start = ((), (), s32[]{:S(2)}) async-start(), calls=%async_computation.11 | async-start | bytes 2064384 | tf_op jit(solution)/shard_map/all_gather | solution.py:96
  8.3 4.4 %collective-permute-start.1 = (bf16[2,2,32,896]{3,2,1,0:T(8,128)(2,1)S(1)}, bf16[2,2,32,896]{3,2,1,0:T(8,128)(2,1)S(1)}, u32[]{:S(2)}, u32[]{:S(2)}) collective-permute-start(bf16[2,2,32,896]{3,2,1,0:T(8,128)(2,1)S(1)} %select_bitcast_fusion), channel_id=1, source_target_pairs={{0,128},{128,0},{1,129},{129,1},{2,130},{130,2},{3,131},{131,3},{4... | collective-permute-start | bytes 688136 | tf_op jit(solution)/shard_map/ppermute | solution.py:20
  12.8 8.6 %collective-permute-start.2 = (bf16[896,1024]{1,0:T(8,128)(2,1)}, bf16[896,1024]{1,0:T(8,128)(2,1)}, u32[]{:S(2)}, u32[]{:S(2)}) collective-permute-start(bf16[896,1024]{1,0:T(8,128)(2,1)} %bitcast.116), channel_id=1, source_target_pairs={{0,128},{128,0},{1,129},{129,1},{2,130},{130,2},{3,131},{131,3},{4... | collective-permute-start | bytes 5505032 | tf_op jit(solution)/shard_map/ppermute | solution.py:20
  15.2 6.2 %copy-start.12 = (bf16[1,896,1024]{2,1,0:T(8,128)(2,1)S(1)}, bf16[1,896,1024]{2,1,0:T(8,128)(2,1)}, u32[]{:S(2)}) copy-start(bf16[1,896,1024]{2,1,0:T(8,128)(2,1)} %param.14) | copy-start | bytes 5505028
  16.4 21.8 %all-to-all-start = ((bf16[16,32,1024]{2,1,0:T(8,128)(2,1)}), bf16[16,32,1024]{2,1,0:T(8,128)(2,1)S(1)}, u32[]{:S(2)}, u32[]{:S(2)}) async-start(bf16[16,32,1024]{2,1,0:T(8,128)(2,1)} %broadcast_in_dim.22), calls=%async_computation | async-start | bytes 2097152 | tf_op jit(solution)/shard_map/all_to_all | solution.py:28
  38.1 4.1 %copy-start.7 = (bf16[16,32,1024]{2,1,0:T(8,128)(2,1)}, bf16[16,32,1024]{2,1,0:T(8,128)(2,1)S(1)}, u32[]{:S(2)}) copy-start(bf16[16,32,1024]{2,1,0:T(8,128)(2,1)S(1)} %all-to-all-done) | copy-start | bytes 3145732
  42.2 32.7 %all-to-all-start.1 = ((bf16[8,64,896]{2,1,0:T(8,128)(2,1)}), bf16[8,64,896]{2,1,0:T(8,128)(2,1)S(1)}, u32[]{:S(2)}, u32[]{:S(2)}) async-start(bf16[8,64,896]{2,1,0:T(8,128)(2,1)} %bitcast.8), calls=%async_computation.1 | async-start | bytes 1835008 | tf_op jit(solution)/shard_map/all_to_all | solution.py:28
  50.4 29.4 %collective-permute-start.4 = (bf16[1024,896]{1,0:T(8,128)(2,1)}, bf16[1024,896]{1,0:T(8,128)(2,1)}, u32[]{:S(2)}, u32[]{:S(2)}) collective-permute-start(bf16[1024,896]{1,0:T(8,128)(2,1)} %bitcast.13), channel_id=1, source_target_pairs={{0,128},{128,0},{1,129},{129,1},{2,130},{130,2},{3,131},{131,3},{4... | collective-permute-start | bytes 5505032 | tf_op jit(solution)/shard_map/ppermute | solution.py:20
  52.6 27.3 %collective-permute-start.5 = (bf16[1024,896]{1,0:T(8,128)(2,1)}, bf16[1024,896]{1,0:T(8,128)(2,1)}, u32[]{:S(2)}, u32[]{:S(2)}) collective-permute-start(bf16[1024,896]{1,0:T(8,128)(2,1)} %bitcast.14), channel_id=1, source_target_pairs={{0,128},{128,0},{1,129},{129,1},{2,130},{130,2},{3,131},{131,3},{4... | collective-permute-start | bytes 5505032 | tf_op jit(solution)/shard_map/ppermute | solution.py:20
  76.1 30.1 %all-to-all-start.2 = ((bf16[8,64,896]{2,1,0:T(8,128)(2,1)}), bf16[8,64,896]{2,1,0:T(8,128)(2,1)S(1)}, u32[]{:S(2)}, u32[]{:S(2)}) async-start(bf16[8,64,896]{2,1,0:T(8,128)(2,1)} %broadcast_in_dim.23), calls=%async_computation.2 | async-start | bytes 1835008 | tf_op jit(solution)/shard_map/all_to_all | solution.py:28
  79.8 26.4 %copy-start = (bf16[2,1,512,896]{3,2,1,0:T(8,128)(2,1)S(1)}, bf16[2,1,512,896]{3,2,1,0:T(8,128)(2,1)}, u32[]{:S(2)}) copy-start(bf16[2,1,512,896]{3,2,1,0:T(8,128)(2,1)} %all-gather.4.cloned.1.call-done) | copy-start | bytes 5505028
  106.2 1.5 copy-start.5
  107.7 1.5 copy-start.6
  115.4 6.8 %copy-start.16 = (f32[1,1024]{1,0:T(1,128)S(1)}, f32[1,1024]{1,0:T(1,128)}, u32[]{:S(2)}) copy-start(f32[1,1024]{1,0:T(1,128)} %param.9) | copy-start | bytes 12292
  115.4 8.6 %copy-start.14 = (bf16[1,64,1024]{2,1,0:T(8,128)(2,1)S(1)}, bf16[1,64,1024]{2,1,0:T(8,128)(2,1)}, u32[]{:S(2)}) copy-start(bf16[1,64,1024]{2,1,0:T(8,128)(2,1)} %param.8) | copy-start | bytes 393220
  115.4 21.3 %all-to-all-start.3 = ((bf16[16,32,1024]{2,1,0:T(8,128)(2,1)}), bf16[16,32,1024]{2,1,0:T(8,128)(2,1)S(1)}, u32[]{:S(2)}, u32[]{:S(2)}) async-start(bf16[16,32,1024]{2,1,0:T(8,128)(2,1)} %bitcast.15), calls=%async_computation.3 | async-start | bytes 2097152 | tf_op jit(solution)/shard_map/all_to_all | solution.py:28
  121.4 49.4 %all-gather.6.cloned.1.call-start = ((), (), s32[]{:S(2)}) async-start(), calls=%async_computation.12 | async-start | bytes 2064384 | tf_op jit(solution)/shard_map/all_gather | solution.py:96
  122.2 2.6 collective-permute-start.3
  124.0 12.9 %collective-permute-start = (bf16[32,1024]{1,0:T(8,128)(2,1)S(1)}, bf16[32,1024]{1,0:T(8,128)(2,1)S(1)}, u32[]{:S(2)}, u32[]{:S(2)}) collective-permute-start(bf16[32,1024]{1,0:T(8,128)(2,1)S(1)} %select_bitcast_fusion.2), channel_id=1, source_target_pairs={{0,128},{128,0},{1,129},{129,1},{2,130},{130,2},{3,131},{131,3},{4... | collective-permute-start | bytes 196616 | tf_op jit(solution)/shard_map/ppermute | solution.py:20
  148.1 18.7 %all-to-all-start.5 = ((bf16[16,32,1024]{2,1,0:T(8,128)(2,1)}), bf16[16,32,1024]{2,1,0:T(8,128)(2,1)S(1)}, u32[]{:S(2)}, u32[]{:S(2)}) async-start(bf16[16,32,1024]{2,1,0:T(8,128)(2,1)} %broadcast_in_dim.25), calls=%async_computation.5 | async-start | bytes 2097152 | tf_op jit(solution)/shard_map/all_to_all | solution.py:28
  166.8 4.1 %copy-start.9 = (bf16[16,32,1024]{2,1,0:T(8,128)(2,1)}, bf16[16,32,1024]{2,1,0:T(8,128)(2,1)S(1)}, u32[]{:S(2)}) copy-start(bf16[16,32,1024]{2,1,0:T(8,128)(2,1)S(1)} %all-to-all-done.5) | copy-start | bytes 3145732
  170.9 26.9 %all-to-all-start.6 = ((bf16[8,64,896]{2,1,0:T(8,128)(2,1)}), bf16[8,64,896]{2,1,0:T(8,128)(2,1)}, u32[]{:S(2)}, u32[]{:S(2)}) async-start(bf16[8,64,896]{2,1,0:T(8,128)(2,1)} %bitcast.117), calls=%async_computation.6 | async-start | bytes 1835008 | tf_op jit(solution)/shard_map/all_to_all | solution.py:28
  175.1 2.4 copy-start.8
  175.1 72.1 %all-gather.8.cloned.1.call-start = ((), (), s32[]{:S(2)}) async-start(), calls=%async_computation.13 | async-start | bytes 2228224 | tf_op jit(solution)/shard_map/all_gather | solution.py:179
  175.9 1.5 copy-start.10
  178.9 25.0 %copy-start.3 = (bf16[2,1,512,896]{3,2,0,1:T(8,128)(2,1)S(1)}, bf16[2,1,512,896]{3,2,0,1:T(8,128)(2,1)}, u32[]{:S(2)}) copy-start(bf16[2,1,512,896]{3,2,0,1:T(8,128)(2,1)} %all-gather.6.cloned.1.call-done) | copy-start | bytes 5505028
  178.9 31.9 %collective-permute-start.7 = (bf16[512,1024]{1,0:T(8,128)(2,1)}, bf16[512,1024]{1,0:T(8,128)(2,1)}, u32[]{:S(2)}, u32[]{:S(2)}) collective-permute-start(bf16[512,1024]{1,0:T(8,128)(2,1)} %get-tuple-element.76), channel_id=1, source_target_pairs={{0,128},{128,0},{1,129},{129,1},{2,130},{130,2},{3,131},{131,3},{4... | collective-permute-start | bytes 3145736 | tf_op jit(solution)/shard_map/ppermute | solution.py:20
  200.2 26.3 %all-to-all-start.7 = ((bf16[8,64,896]{2,1,0:T(8,128)(2,1)}), bf16[8,64,896]{2,1,0:T(8,128)(2,1)S(1)}, u32[]{:S(2)}, u32[]{:S(2)}) async-start(bf16[8,64,896]{2,1,0:T(8,128)(2,1)} %broadcast_in_dim.26), calls=%async_computation.7 | async-start | bytes 1835008 | tf_op jit(solution)/shard_map/all_to_all | solution.py:28
  203.9 1.2 copy-start.11
  205.1 6.6 %copy-start.13 = (bf16[512,1024]{1,0:T(8,128)(2,1)S(1)}, bf16[512,1024]{1,0:T(8,128)(2,1)}, u32[]{:S(2)}) copy-start(bf16[512,1024]{1,0:T(8,128)(2,1)} %get-tuple-element.75) | copy-start | bytes 3145732
  205.3 6.4 %collective-permute-start.6 = (bf16[512,896]{1,0:T(8,128)(2,1)S(1)}, bf16[512,896]{1,0:T(8,128)(2,1)S(1)}, u32[]{:S(2)}, u32[]{:S(2)}) collective-permute-start(bf16[512,896]{1,0:T(8,128)(2,1)S(1)} %get-tuple-element.78), channel_id=1, source_target_pairs={{0,128},{128,0},{1,129},{129,1},{2,130},{130,2},{3,131},{131,3},{4... | collective-permute-start | bytes 2752520 | tf_op jit(solution)/shard_map/ppermute | solution.py:20
  209.6 44.7 %collective-permute-start.13 = (bf16[512,896]{1,0:T(8,128)(2,1)}, bf16[512,896]{1,0:T(8,128)(2,1)}, u32[]{:S(2)}, u32[]{:S(2)}) collective-permute-start(bf16[512,896]{1,0:T(8,128)(2,1)} %get-tuple-element.60), channel_id=1, source_target_pairs={{0,128},{1,129},{2,130},{3,131},{4,132},{5,133},{6,134},{7,135},{8... | collective-permute-start | bytes 2752520 | tf_op jit(solution)/shard_map/ppermute | solution.py:148
  211.7 14.8 %copy-start.1 = (bf16[1024,896]{1,0:T(8,128)(2,1)S(1)}, bf16[1024,896]{1,0:T(8,128)(2,1)}, u32[]{:S(2)}) copy-start(bf16[1024,896]{1,0:T(8,128)(2,1)} %get-tuple-element.52.up_w) | copy-start | bytes 5505028
  226.5 1.5 copy-start.2
  228.0 1.5 copy-start.4
  235.7 18.6 %collective-permute-start.12 = (bf16[512,896]{1,0:T(8,128)(2,1)}, bf16[512,896]{1,0:T(8,128)(2,1)}, u32[]{:S(2)}, u32[]{:S(2)}) collective-permute-start(bf16[512,896]{1,0:T(8,128)(2,1)} %get-tuple-element.58), channel_id=1, source_target_pairs={{128,0},{129,1},{130,2},{131,3},{132,4},{133,5},{134,6},{135,7},{1... | collective-permute-start | bytes 2752520 | tf_op jit(solution)/shard_map/ppermute | solution.py:148
  242.7 12.9 %collective-permute-start.11 = (bf16[512,896]{1,0:T(8,128)(2,1)}, bf16[512,896]{1,0:T(8,128)(2,1)S(1)}, u32[]{:S(2)}, u32[]{:S(2)}) collective-permute-start(bf16[512,896]{1,0:T(8,128)(2,1)} %get-tuple-element.57), channel_id=1, source_target_pairs={{0,128},{1,129},{2,130},{3,131},{4,132},{5,133},{6,134},{7,135},{8... | collective-permute-start | bytes 2752520 | tf_op jit(solution)/shard_map/ppermute | solution.py:148
  244.0 11.6 %collective-permute-start.10 = (bf16[512,896]{1,0:T(8,128)(2,1)}, bf16[512,896]{1,0:T(8,128)(2,1)S(1)}, u32[]{:S(2)}, u32[]{:S(2)}) collective-permute-start(bf16[512,896]{1,0:T(8,128)(2,1)} %get-tuple-element.56), channel_id=1, source_target_pairs={{128,0},{129,1},{130,2},{131,3},{132,4},{133,5},{134,6},{135,7},{1... | collective-permute-start | bytes 2752520 | tf_op jit(solution)/shard_map/ppermute | solution.py:148
  247.3 24.5 %all-to-all-start.8 = ((bf16[16,32,1024]{2,1,0:T(8,128)(2,1)}), bf16[16,32,1024]{2,1,0:T(8,128)(2,1)S(1)}, u32[]{:S(2)}, u32[]{:S(2)}) async-start(bf16[16,32,1024]{2,1,0:T(8,128)(2,1)} %bitcast.34), calls=%async_computation.8 | async-start | bytes 2097152 | tf_op jit(solution)/shard_map/all_to_all | solution.py:28
  255.6 1.6 copy-start.17
  272.7 9.7 %all-to-all-start.9 = ((f32[8,1,32]{2,1,0:T(1,128)}), f32[8,1,32]{2,1,0:T(1,128)S(1)}, u32[]{:S(2)}, u32[]{:S(2)}) async-start(f32[8,1,32]{2,1,0:T(1,128)} %broadcast_in_dim.27), calls=%async_computation.9 | async-start | bytes 8192 | tf_op jit(solution)/shard_map/all_to_all | solution.py:28
  283.1 10.3 %all-to-all-start.10 = ((f32[16,2,1024]{2,1,0:T(2,128)}), f32[16,2,1024]{2,1,0:T(2,128)S(1)}, u32[]{:S(2)}, u32[]{:S(2)}) async-start(f32[16,2,1024]{2,1,0:T(2,128)} %broadcast_in_dim.28), calls=%async_computation.10 | async-start | bytes 262144 | tf_op jit(solution)/shard_map/all_to_all | solution.py:28
  286.8 9.5 %collective-permute-start.8 = (bf16[32,1024]{1,0:T(8,128)(2,1)S(1)}, bf16[32,1024]{1,0:T(8,128)(2,1)S(1)}, u32[]{:S(2)}, u32[]{:S(2)}) collective-permute-start(bf16[32,1024]{1,0:T(8,128)(2,1)S(1)} %get-tuple-element.82), channel_id=1, source_target_pairs={{0,128},{128,0},{1,129},{129,1},{2,130},{130,2},{3,131},{131,3},{4... | collective-permute-start | bytes 196616 | tf_op jit(solution)/shard_map/ppermute | solution.py:20
  293.4 3.7 %collective-permute-start.9 = (f32[1024]{0:T(1024)S(1)}, f32[1024]{0:T(1024)S(1)}, u32[]{:S(2)}, u32[]{:S(2)}) collective-permute-start(f32[1024]{0:T(1024)S(1)} %bitcast.135), channel_id=1, source_target_pairs={{0,128},{128,0},{1,129},{129,1},{2,130},{130,2},{3,131},{131,3},{4... | collective-permute-start | bytes 12296 | tf_op jit(solution)/shard_map/ppermute | solution.py:20
Sparse Core Ops, SparseCore 0:
  15.3 37.7 all-gather.3
  124.1 34.4 all-gather.5
  179.0 50.5 all-gather.7
